TPU v7x, 32 devices: a whole 2x2x4 slice. The times are simulated.
32 devices in a mesh: group: 8 (over y, x, core), expert: 4 (over z).
Axes of the slice: x: 2, y: 2, z: 4, core: 2. Of those that a mesh axis runs over, the one named last changes fastest.
Arguments:
- tokens: bfloat16 [4096, 1536], P(('group', 'expert')), may hold values from -6 to 6
- gate_train: float32 [8, 1536, 512], P('expert', 'group'), may hold values from -0.15625 to 0.15625
- up_train: float32 [8, 1536, 512], P('expert', 'group'), may hold values from -0.15625 to 0.15625
- down_train: float32 [8, 512, 1536], P('expert', None, 'group'), may hold values from -0.25 to 0.25
- routes: int32 [4096, 6], P(('group', 'expert')), may hold values from 0 to 7, as said below
- route_scores: float32 [4096, 6], P(('group', 'expert')), may hold values from 0.05 to 1
- live: int32 [4096], P(('group', 'expert')), may hold values from 0 to 1
Outputs:
- moe_out: bfloat16 [4096, 1536], P(('group', 'expert'))
Inputs may be any that keep to these rules, and one draw needn't show every extreme that they name: `routes`: each row names 6 different experts; one expert, the same on every device, is named by at least 96 live rows among each device's 128 rows.
All inputs are finite; a program needn't handle non-finite values.
Results may differ from a plain program's by a relative error of at most 0.0075.
Values may be sent and summed in bfloat16 or wider, within the bound.
A program may use at most 64 MiB of HBM per device.

v0:
```python
import jax
import jax.numpy as jnp
from jax import lax
from jax.sharding import PartitionSpec as P


def local(tokens, gate_train, up_train, down_train, routes, route_scores, live):
    local_experts = gate_train.shape[0]
    hidden_width = gate_train.shape[2]
    holders = lax.axis_size("expert")
    experts = local_experts * holders
    tok_dev, model_width = tokens.shape
    top_count = routes.shape[1]
    capacity = tok_dev * top_count // experts
    total_slots = experts * capacity
    route_share = route_scores / jnp.sum(route_scores, axis=1, keepdims=True)
    flat_route = routes.reshape(-1)
    flat_live = jnp.repeat(live, top_count)
    expert_ids = jnp.arange(experts, dtype=jnp.int32)
    onehot = ((flat_route[:, None] == expert_ids[None, :]) & (flat_live[:, None] > 0)).astype(
        jnp.int32
    )
    earlier = jnp.cumsum(onehot, axis=0) - onehot
    slot_index = jnp.sum(earlier * onehot, axis=1)
    kept_mask = (flat_live > 0) & (slot_index < capacity)
    target = jnp.where(kept_mask, flat_route * capacity + slot_index, total_slots)
    anchor = jnp.arange(tok_dev * top_count, dtype=jnp.int32) // top_count
    source_row = jnp.zeros((total_slots,), jnp.int32).at[target].set(anchor, mode="drop")
    filled = jnp.zeros((total_slots,), jnp.int32).at[target].set(1, mode="drop")
    outgoing = jnp.where(filled[:, None] > 0, tokens[source_row], jnp.zeros((), jnp.bfloat16))
    outgoing = outgoing.reshape(holders, local_experts * capacity, model_width)
    incoming = lax.all_to_all(outgoing, "expert", split_axis=0, concat_axis=0, tiled=True)
    incoming = incoming.reshape(holders, local_experts, capacity, model_width)
    gate_up_local = jnp.concatenate([gate_train, up_train], axis=2).astype(jnp.bfloat16)
    down_local = down_train.astype(jnp.bfloat16)
    gate_up_w, down_w = (
        lax.all_gather(gate_up_local, "group", axis=1, tiled=True),
        lax.all_gather(down_local, "group", axis=2, tiled=True),
    )
    gate_up = jnp.einsum("sjcd,jdf->sjcf", incoming, gate_up_w, preferred_element_type=jnp.float32)
    hidden = (jax.nn.silu(gate_up[..., :hidden_width]) * gate_up[..., hidden_width:]).astype(
        jnp.bfloat16
    )
    expert_out = jnp.einsum("sjcf,jfd->sjcd", hidden, down_w, preferred_element_type=jnp.float32)
    expert_rows = expert_out.astype(jnp.bfloat16).reshape(
        holders, local_experts * capacity, model_width
    )
    returned = lax.all_to_all(
        expert_rows, "expert", split_axis=0, concat_axis=0, tiled=True
    ).reshape(total_slots, model_width)
    picked = returned[jnp.minimum(target, total_slots - 1)]
    weight = jnp.where(kept_mask, route_share.reshape(-1), 0.0)
    combined = jnp.sum(
        picked.reshape(tok_dev, top_count, model_width).astype(jnp.float32)
        * weight.reshape(tok_dev, top_count, 1),
        axis=1,
    )
    return combined.astype(jnp.bfloat16)


def solution(mesh):
    in_specs = (
        P(("group", "expert"), None),
        P("expert", "group", None),
        P("expert", "group", None),
        P("expert", None, "group"),
        P(("group", "expert"), None),
        P(("group", "expert"), None),
        P(("group", "expert")),
    )
    out_specs = P(("group", "expert"), None)
    return jax.shard_map(local, mesh=mesh, in_specs=in_specs, out_specs=out_specs, check_vma=False)
```

profile of v0, /device:TPU:0, one launch (start us, length us, event | category | flops | bytes accessed | tf_op | source)
XLA Modules:
  0.0 179.2 jit_solution(3360856335421369290)
XLA Ops:
  6.5 1.3 convert.7
  7.8 1.2 convert.8
  9.0 1.0 pad_maximum_fusion
  10.1 0.8 convert_element_type.32
  11.1 0.2 gt.41
  11.2 0.1 gt.40
  11.8 0.1 gt.39
  12.0 1.7 reduce-window.6
  13.9 0.2 reduce-window.9
  14.5 3.4 %scatter_custom_fusion.1 = s32[768]{0:T(1024)S(1)} fusion(s32[768]{0:T(1024)S(1)} %get-tuple-element.6, s32[768]{0:T(1024)S(1)} %add_select_fusion, s32[]{:T(128)} %constant.11.clone.1), kind=kCustom, calls=%fused_computation.43 | custom fusion | bytes 3076 | tf_op jit(solution)/shard_map/scatter | solution.py:28
  17.9 3.4 %scatter_custom_fusion = s32[768]{0:T(1024)S(1)} fusion(s32[768]{0:T(1024)S(1)} %get-tuple-element.6, s32[768]{0:T(1024)S(1)} %broadcast.166, s32[]{:T(128)} %constant.11.clone.1), kind=kCustom, calls=%fused_computation.46 | custom fusion | bytes 3076 | tf_op jit(solution)/shard_map/scatter | solution.py:29
  21.4 2.9 %gather_fusion = bf16[768,1536]{1,0:T(8,128)(2,1)S(1)} fusion(bf16[128,1536]{1,0:T(8,128)(2,1)S(1)} %copy-done, s32[1024]{0:T(1024)S(1)} %pad_clamp_fusion.1), kind=kCustom, calls=%fused_computation | custom fusion | bytes 4721664 | tf_op jit(solution)/shard_map/gather | solution.py:30
  24.4 0.2 broadcast_select_fusion
  24.6 59.9 %all_to_all.10 = bf16[4,192,1536]{2,1,0:T(8,128)(2,1)S(1)} all-to-all(bf16[4,192,1536]{2,1,0:T(8,128)(2,1)S(1)} %broadcast_select_fusion), channel_id=1, replica_groups=mesh['group'=8,'expert'=4] {'expert'}, dimensions={0} | all-to-all | bytes 4718592 | tf_op jit(solution)/shard_map/all_to_all | solution.py:32
  84.5 7.1 %fusion.7 = f32[4,2,96,1024]{3,2,0,1:T(8,128)} fusion(bf16[4,2,96,1536]{3,2,1,0:T(8,128)(2,1)S(1)} %bitcast.35, bf16[2,1536,1024]{2,1,0:T(8,128)(2,1)} %all-gather.3.cloned.1.call-done), kind=kOutput, calls=%fused_computation.12 | convolution fusion | flops 2415919104 | bytes 11796480 | tf_op jit(solution)/shard_map/sjcd,jdf->sjcf/dot_general | solution.py:40
  91.6 1.1 all-gather.5.cloned.1.call-done
  92.7 4.3 %fusion.3 = bf16[4,2,96,1536]{3,2,0,1:T(8,128)(2,1)S(1)} fusion(bf16[2,512,1536]{1,2,0:T(8,128)(2,1)} %all-gather.5.cloned.1.call-done, f32[4,2,96,1024]{3,2,0,1:T(8,128)} %fusion.7), kind=kOutput, calls=%fused_computation.9 | convolution fusion | flops 1211498496 | bytes 8650752 | tf_op jit(solution)/shard_map/sjcf,jfd->sjcd/dot_general | solution.py:44
  97.0 1.7 copy.29
  98.6 4.7 %all-to-all-start.1 = ((bf16[4,192,1536]{2,1,0:T(8,128)(2,1)}), bf16[4,192,1536]{2,1,0:T(8,128)(2,1)S(1)}, u32[]{:S(2)}, u32[]{:S(2)}) async-start(bf16[4,192,1536]{2,1,0:T(8,128)(2,1)} %bitcast.33), calls=%async_computation.1 | async-start | bytes 4718592 | tf_op jit(solution)/shard_map/all_to_all | solution.py:48
  103.4 0.2 lt.50
  103.8 53.8 %all-to-all-done.1 = bf16[4,192,1536]{2,1,0:T(8,128)(2,1)S(1)} async-done(((bf16[4,192,1536]{2,1,0:T(8,128)(2,1)}), bf16[4,192,1536]{2,1,0:T(8,128)(2,1)S(1)}, u32[]{:S(2)}, u32[]{:S(2)}) %all-to-all-start.1) | async-done | bytes 2359328 | tf_op jit(solution)/shard_map/all_to_all | solution.py:48
  157.6 3.9 %gather_fusion.1 = bf16[768,1536]{1,0:T(8,128)(2,1)} fusion(bf16[768,1536]{1,0:T(8,128)(2,1)S(1)} %bitcast.32, s32[1024]{0:T(1024)S(1)} %pad_clamp_fusion), kind=kCustom, calls=%fused_computation.1 | custom fusion | bytes 4721664 | tf_op jit(solution)/shard_map/gather | solution.py:51
  161.5 5.0 %reshape.148 = f32[128,6,1536]{2,1,0:T(8,128)} reshape(bf16[768,1536]{1,0:T(8,128)(2,1)} %gather_fusion.1) | data formatting | bytes 7077888 | tf_op jit(solution)/shard_map/convert_element_type | solution.py:54
  166.5 5.9 %multiply_reduce_fusion = bf16[128,1536]{1,0:T(8,128)(2,1)} fusion(f32[128,6,1536]{2,1,0:T(8,128)} %reshape.148, f32[128,6]{1,0:T(8,128)S(1)} %copy.31), kind=kLoop, calls=%fused_computation.6 | loop fusion | flops 2162688 | bytes 5114880 | tf_op jit(solution)/shard_map/reduce_sum | solution.py:53
  (41 shorter events, 1.6 us)
Async XLA Ops:
  6.5 14.9 %copy-start = (bf16[128,1536]{1,0:T(8,128)(2,1)S(1)}, bf16[128,1536]{1,0:T(8,128)(2,1)}, u32[]{:S(2)}) copy-start(bf16[128,1536]{1,0:T(8,128)(2,1)} %param.7) | copy-start | bytes 1179652
  6.5 3.6 %copy-start.1 = (f32[2,512,192]{1,2,0:T(8,128)S(1)}, f32[2,512,192]{1,2,0:T(8,128)}, u32[]{:S(2)}) copy-start(f32[2,512,192]{1,2,0:T(8,128)} %param.10) | copy-start | bytes 2359300
  6.5 78.0 %all-gather.3.cloned.1.call-start = ((), (), s32[]{:S(2)}) async-start(), calls=%async_computation.2 | async-start | bytes 7077888 | tf_op jit(solution)/shard_map/all_gather | solution.py:37
  7.8 3.1 %copy-start.4 = (s32[128]{0:T(128)S(1)}, s32[128]{0:T(128)}, u32[]{:S(2)}) copy-start(s32[128]{0:T(128)} %param.13) | copy-start | bytes 1540
  7.8 3.5 %copy-start.2 = (s32[128,6]{0,1:T(8,128)S(1)}, s32[128,6]{0,1:T(8,128)}, u32[]{:S(2)}) copy-start(s32[128,6]{0,1:T(8,128)} %param.11) | copy-start | bytes 9220
  10.1 82.6 %all-gather.5.cloned.1.call-start = ((), (), s32[]{:S(2)}) async-start(), calls=%async_computation.3 | async-start | bytes 3538944 | tf_op jit(solution)/shard_map/all_gather | solution.py:38
  98.6 5.0 %copy-start.3 = (f32[128,6]{0,1:T(8,128)S(1)}, f32[128,6]{0,1:T(8,128)}, u32[]{:S(2)}) copy-start(f32[128,6]{0,1:T(8,128)} %param.12) | copy-start | bytes 9220
  98.6 59.0 %all-to-all-start.1 = ((bf16[4,192,1536]{2,1,0:T(8,128)(2,1)}), bf16[4,192,1536]{2,1,0:T(8,128)(2,1)S(1)}, u32[]{:S(2)}, u32[]{:S(2)}) async-start(bf16[4,192,1536]{2,1,0:T(8,128)(2,1)} %bitcast.33), calls=%async_computation.1 | async-start | bytes 4718592 | tf_op jit(solution)/shard_map/all_to_all | solution.py:48
Sparse Core Ops, SparseCore 0:
  10.2 48.2 all-gather.2
  60.3 32.3 all-gather.4
where the time goes:
time: 180 us; the launch traced here: 179 us
  blocking collectives  59.9 us (33%)
  waiting for transfers between devices  54.9 us (30%)
  local copies, waits for them, and re-layouts  22.1 us (12%)
  between operations  13.6 us (8%)
  other arithmetic  12.5 us (7%)
  matrix products  11.4 us (6%)
  starting transfers between devices  4.77 us (3%)
    all_to_all x1, blocking collectives, local(): lax.all_to_all(outgoing, 'expert', split_axis=0, concat_axis=0, tiled=True)  59.9 us
    all_to_all x1, waiting for transfers between devices, local(): lax.all_to_all(expert_rows, 'expert', split_axis=0, concat_axis=0, tiled=...  53.8 us
    dot_general x1, matrix products, local(): jnp.einsum('sjcd,jdf->sjcf', incoming, gate_up_w, preferred_element_type=...  7.09 us
    reduce_sum x1, other arithmetic, local(): jnp.sum(picked.reshape(tok_dev, top_count, model_width).astype(jnp.float3...  5.92 us
    convert_element_type x1, local copies, waits for them, and re-layouts, local(): picked.reshape(tok_dev, top_count, model_width).astype(jnp.float32)  4.98 us
    all_to_all x1, starting transfers between devices, local(): lax.all_to_all(expert_rows, 'expert', split_axis=0, concat_axis=0, tiled=...  4.73 us
    another operation x4, other arithmetic  4.34 us
    dot_general x1, matrix products, local(): jnp.einsum('sjcf,jfd->sjcd', hidden, down_w, preferred_element_type=jnp.f...  4.27 us
  transfers between devices with their start and end apart: 3, of which 2 were waited for; matrix products, arithmetic and copies ran while one was open for 12% of the time, Pallas kernels for 0%

commit v1 on v0

v1 whole, which is shorter than its diff:
```python
import functools

import jax
import jax.numpy as jnp
from jax import lax
from jax.experimental import pallas as pl
from jax.experimental.pallas import tpu as pltpu
from jax.sharding import PartitionSpec as P

MESH = pl.DeviceIdType.MESH
F32, BF16 = jnp.float32, jnp.bfloat16
PAIR = (((1,), (1,)), ((), ()))


def xor(value, mask):
    bit = 1
    while bit <= mask:
        if mask & bit:
            value = value + bit * (1 - 2 * ((value // bit) % 2))
        bit *= 2
    return value


def kernel(
    n_group, n_hold, capacity,
    tokens, gate, up, down, routes, scores, live, out,
    w_gu, w_down, tok_all, share_out, share_in, hidden, stage, back, flip, down_flip,
    gu_send, gu_recv, down_send, down_recv, tok_send, tok_recv, share_send, share_recv,
    ret_send, ret_recv,
):
    local, rows, ff = gate.shape
    block, width = tokens.shape
    top = routes.shape[1]
    experts = local * n_hold
    chips = n_group // 2
    square = chips == 4
    me, holder = lax.axis_index("group"), lax.axis_index("expert")
    chip = me // 2
    sibling = xor(me, 1)

    def device(group, expert):
        return (group, expert)

    def peer(d):
        return lax.rem(holder + d, n_hold)

    def origin(d):
        return lax.rem(holder + n_hold - d, n_hold)

    near = (1, 2) if square else tuple(range(1, chips))
    barrier = pltpu.get_barrier_semaphore()
    partners = [device(xor(me, 2 * j), holder) for j in near] + [device(sibling, holder)]
    partners += [device(me, peer(d)) for d in range(1, n_hold)]
    for partner in partners:
        pl.semaphore_signal(barrier, inc=1, device_id=partner, device_id_type=MESH)

    mine = pl.multiple_of(me * rows, rows)
    for e in range(local):
        w_gu[e, pl.ds(mine, rows), :ff] = gate[e].astype(BF16)
        w_gu[e, pl.ds(mine, rows), ff:] = up[e].astype(BF16)
    pl.semaphore_wait(barrier, len(partners))

    started = []

    def start(src, dst, send, recv, target):
        copy = pltpu.make_async_remote_copy(
            src_ref=src, dst_ref=dst, send_sem=send, recv_sem=recv,
            device_id=target, device_id_type=MESH,
        )
        copy.start()
        started.append(copy)

    halves = 2 if square else 1
    half_rows = rows // halves

    def piece(kind, key, owner):
        base = pl.multiple_of(owner * rows + key[-1] * half_rows, half_rows)
        if kind == "gu":
            return w_gu.at[key[0], pl.ds(base, half_rows), :]
        return w_down.at[pl.ds(base, half_rows), :]

    def sems(kind, key):
        if kind == "gu":
            index = key[0] * halves + key[1]
            return gu_send, gu_recv, index
        return down_send, down_recv, key[0]

    def send_piece(kind, key, owner, slot, target):
        send, recv, index = sems(kind, key)
        ref = piece(kind, key, owner)
        start(ref, ref, send.at[index, slot], recv.at[index, slot], device(target, holder))

    def wait_piece(kind, key, owner, slot):
        send, recv, index = sems(kind, key)
        ref = piece(kind, key, owner)
        pltpu.make_async_remote_copy(
            src_ref=ref, dst_ref=ref, send_sem=send.at[index, slot], recv_sem=recv.at[index, slot],
            device_id=device(sibling, holder), device_id_type=MESH,
        ).wait_recv()

    def send_own(kind, keys):
        for key in keys:
            order = near if key[-1] == 0 else near[::-1]
            for j in order:
                send_piece(kind, key, me, j, xor(me, 2 * j))
        for key in keys:
            send_piece(kind, key, me, chips, sibling)

    def service_near(kind, keys):
        for key in keys:
            for j in near:
                owner = xor(me, 2 * j)
                wait_piece(kind, key, owner, j)
                if square and (j == 1) == (key[-1] == 0):
                    send_piece(kind, key, owner, 3, xor(me, 2 * (3 - j)))
                send_piece(kind, key, owner, chips + j, sibling)

    def service_far(kind, keys):
        if square:
            for key in keys:
                owner = xor(me, 6)
                wait_piece(kind, key, owner, 3)
                send_piece(kind, key, owner, chips + 3, sibling)

    def wait_sibling(kind, keys, j):
        for key in keys:
            wait_piece(kind, key, xor(sibling, 2 * j), chips + j)

    gu_keys = [[(e, a) for a in range(halves)] for e in range(local)]
    down_keys = [(a,) for a in range(halves)]

    send_own("gu", gu_keys[0])
    for d in range(1, n_hold):
        start(tokens, tok_all.at[d], tok_send.at[d], tok_recv.at[d], device(me, peer(d)))
    for e in range(1, local):
        send_own("gu", gu_keys[e])

    flip[...] = jnp.zeros_like(flip)
    flip[:, :top] = routes[...].astype(F32)
    flip[:, 8:8 + top] = scores[...]
    turned = flip[...].T
    named_expert = turned[:top]
    chosen = turned[8:8 + top]
    chosen = chosen / jnp.sum(chosen, axis=0, keepdims=True)
    expert_id = lax.broadcasted_iota(jnp.int32, (experts, block), 0).astype(F32)
    weight = jnp.zeros((experts, block), F32)
    named = jnp.zeros((experts, block), F32)
    for k in range(top):
        hit = named_expert[k:k + 1] == expert_id
        weight = weight + jnp.where(hit, chosen[k:k + 1], 0.0)
        named = named + jnp.where(hit, 1.0, 0.0)
    alive = (live[...] > 0).astype(F32)
    named = named * alive
    before = (
        lax.broadcasted_iota(jnp.int32, (block, block), 0)
        < lax.broadcasted_iota(jnp.int32, (block, block), 1)
    ).astype(BF16)
    earlier = jnp.dot(named.astype(BF16), before, preferred_element_type=F32)
    weight = jnp.where((earlier < capacity) & (alive > 0), weight, 0.0)
    share_out[...] = jnp.zeros_like(share_out)
    for p in range(n_hold):
        share_out[p, :local, :] = weight[p * local:(p + 1) * local]
    for d in range(1, n_hold):
        start(
            share_out.at[peer(d)], share_in.at[d], share_send.at[d], share_recv.at[d],
            device(me, peer(d)),
        )

    for e in range(local):
        down_flip[:, :rows] = down[e]
        w_down[pl.ds(mine, rows), e * ff:(e + 1) * ff] = (
            down_flip[...].T[:rows].astype(BF16)
        )
    tok_all[0] = tokens[...]
    share_in[0] = share_out[holder]

    for e in range(local):
        service_near("gu", gu_keys[e])
        if e > 0:
            service_far("gu", gu_keys[e - 1])
    send_own("down", down_keys)
    service_far("gu", gu_keys[local - 1])
    for e in range(local):
        for j in range(chips):
            wait_sibling("gu", gu_keys[e], j)

    tile = 256
    per_group = 2

    def wait_tokens(d):
        for src, dst, send, recv in (
            (tokens, tok_all.at[d], tok_send.at[d], tok_recv.at[d]),
            (share_out.at[0], share_in.at[d], share_send.at[d], share_recv.at[d]),
        ):
            pltpu.make_async_remote_copy(
                src_ref=src, dst_ref=dst, send_sem=send, recv_sem=recv,
                device_id=device(sibling, holder), device_id_type=MESH,
            ).wait_recv()

    def hidden_group(first):
        count = per_group * block
        flip[: per_group * 8] = share_in[first:first + per_group].reshape(per_group * 8, block)
        columns = flip[...].T
        picked = tok_all[first:first + per_group].reshape(count, width)
        for e in range(local):
            scale = jnp.concatenate(
                [columns[:, i * 8 + e:i * 8 + e + 1] for i in range(per_group)], axis=0
            )

            def body(j, carry):
                at = pl.multiple_of(j * tile, tile)
                g = jnp.dot(picked, w_gu[e, :, pl.ds(at, tile)], preferred_element_type=F32)
                u = jnp.dot(
                    picked, w_gu[e, :, pl.ds(pl.multiple_of(ff + at, tile), tile)],
                    preferred_element_type=F32,
                )
                value = (g / (1.0 + jnp.exp(-g))) * u * scale
                hidden[first * block:first * block + count,
                       pl.ds(pl.multiple_of(e * ff + at, tile), tile)] = value.astype(BF16)
                return carry

            lax.fori_loop(0, ff // tile, body, 0)

    for first in range(0, n_hold, per_group):
        if first == per_group or n_hold == per_group:
            service_near("down", down_keys)
        for d in range(first, first + per_group):
            if d > 0:
                wait_tokens(d)
        hidden_group(first)

    parts, piece_width = back.shape[1], back.shape[3]

    def column(part):
        if parts == 1:
            return 0
        return pl.multiple_of(xor(chip, part) * piece_width, piece_width)

    for part in range(parts):
        if parts == 1:
            service_far("down", down_keys)
            for j in range(chips):
                wait_sibling("down", down_keys, j)
        else:
            if part == min(2, parts - 1):
                service_far("down", down_keys)
            wait_sibling("down", down_keys, part)
        at = column(part)
        for first in range(0, n_hold, 4):
            count = min(4, n_hold - first)
            value = lax.dot_general(
                hidden[first * block:(first + count) * block, :],
                w_down[pl.ds(at, piece_width), :], PAIR, preferred_element_type=F32,
            )
            stage[first:first + count, part] = value.astype(BF16).reshape(
                count, block, piece_width
            )
        for d in range(n_hold - 1, 0, -1):
            start(
                stage.at[d, part], back.at[d, part], ret_send.at[d, part], ret_recv.at[d, part],
                device(me, origin(d)),
            )

    for part in range(parts):
        total = stage[0, part].astype(F32)
        for d in range(1, n_hold):
            pltpu.make_async_remote_copy(
                src_ref=stage.at[d, part], dst_ref=back.at[d, part],
                send_sem=ret_send.at[d, part], recv_sem=ret_recv.at[d, part],
                device_id=device(sibling, holder), device_id_type=MESH,
            ).wait_recv()
            total = total + back[d, part].astype(F32)
        out[:, pl.ds(column(part), piece_width)] = total.astype(BF16)

    for copy in started:
        copy.wait_send()


def local(n_group, n_hold, tokens, gate, up, down, routes, scores, live):
    experts_here, rows, ff = gate.shape
    block, width = tokens.shape
    top = routes.shape[1]
    capacity = block * top // (experts_here * n_hold)
    chips = n_group // 2
    halves = 2 if chips == 4 else 1
    parts = chips if (2 * rows) % 128 == 0 else 1
    padded = -(-rows // 128) * 128
    dma = pltpu.SemaphoreType.DMA
    vmem = pl.BlockSpec(memory_space=pltpu.VMEM)
    return pl.pallas_call(
        functools.partial(kernel, n_group, n_hold, capacity),
        out_shape=jax.ShapeDtypeStruct((block, width), BF16),
        in_specs=[vmem] * 7,
        out_specs=vmem,
        scratch_shapes=[
            pltpu.VMEM((experts_here, width, 2 * ff), BF16),
            pltpu.VMEM((width, experts_here * ff), BF16),
            pltpu.VMEM((n_hold, block, width), BF16),
            pltpu.VMEM((n_hold, 8, block), F32),
            pltpu.VMEM((n_hold, 8, block), F32),
            pltpu.VMEM((n_hold * block, experts_here * ff), BF16),
            pltpu.VMEM((n_hold, parts, block, width // parts), BF16),
            pltpu.VMEM((n_hold, parts, block, width // parts), BF16),
            pltpu.VMEM((128, 128), F32),
            pltpu.VMEM((ff, padded), F32),
            dma((experts_here * halves, 2 * chips)),
            dma((experts_here * halves, 2 * chips)),
            dma((halves, 2 * chips)),
            dma((halves, 2 * chips)),
            dma((n_hold,)),
            dma((n_hold,)),
            dma((n_hold,)),
            dma((n_hold,)),
            dma((n_hold, parts)),
            dma((n_hold, parts)),
        ],
        compiler_params=pltpu.CompilerParams(
            collective_id=0, has_side_effects=True, vmem_limit_bytes=56 * 2**20
        ),
    )(tokens, gate, up, down, routes, scores, live.reshape(1, block))


def solution(mesh):
    in_specs = (
        P(("group", "expert"), None),
        P("expert", "group", None),
        P("expert", "group", None),
        P("expert", None, "group"),
        P(("group", "expert"), None),
        P(("group", "expert"), None),
        P(("group", "expert")),
    )
    out_specs = P(("group", "expert"), None)
    body = functools.partial(local, mesh.shape["group"], mesh.shape["expert"])
    return jax.shard_map(body, mesh=mesh, in_specs=in_specs, out_specs=out_specs, check_vma=False)
```

time: 180 us -> 88.9 us (0.49)
  Pallas kernels: 0 us -> 82.3 us
  blocking collectives: 59.9 us -> 0 us
  waiting for transfers between devices: 54.9 us -> 0 us
  local copies, waits for them, and re-layouts: 22.1 us -> 6.39 us
  between operations: 13.6 us -> 0.01 us
  other arithmetic: 12.5 us -> 0 us
  matrix products: 11.4 us -> 0 us
  starting transfers between devices: 4.77 us -> 0 us
    pallas_call x0 -> x1, Pallas kernels: none -> 82.3 us  [local(): pl.pallas_call(functools.partial(kernel, n_group, n_hold, capacity), out_...]
    all_to_all x1 -> x0, blocking collectives: 59.9 us -> none  [local(): lax.all_to_all(outgoing, 'expert', split_axis=0, concat_axis=0, tiled=True)]
    all_to_all x1 -> x0, waiting for transfers between devices: 53.8 us -> none  [local(): lax.all_to_all(expert_rows, 'expert', split_axis=0, concat_axis=0, tiled=...]
    dot_general x2 -> x0, matrix products: 11.4 us -> none  [the longest x1 7.09 us: local(): jnp.einsum('sjcd,jdf->sjcf', incoming, gate_up_w, preferred_element_type=...]
    gather x2 -> x0, local copies, waits for them, and re-layouts: 6.79 us -> none  [the longest x1 3.87 us: local(): picked = returned[jnp.minimum(target, total_slots - 1)]]
    scatter x2 -> x0, local copies, waits for them, and re-layouts: 6.76 us -> none  [the longest x1 3.38 us: local(): jnp.zeros((total_slots,), jnp.int32).at[target].set(anchor, mode='drop')]
    convert_element_type x2 -> x0, local copies, waits for them, and re-layouts: 6.64 us -> none  [the longest x1 4.98 us: local(): picked.reshape(tok_dev, top_count, model_width).astype(jnp.float32)]
    unnamed x11 -> x6, local copies, waits for them, and re-layouts: 0.14 us -> 6.39 us
  transfers between devices with their start and end apart: 3 -> 0, of which waited for: 2 -> 0; matrix products, arithmetic and copies ran while one was open for 12% -> 0% of each run, Pallas kernels for 0% -> 0%
where the time goes in v1:
time: 88.9 us; the launch traced here: 88.7 us
  Pallas kernels  82.3 us (93%)
  local copies, waits for them, and re-layouts  6.39 us (7%)
    pallas_call x1, Pallas kernels, local(): pl.pallas_call(functools.partial(kernel, n_group, n_hold, capacity), out_...  82.3 us
    unnamed x6, local copies, waits for them, and re-layouts  6.39 us

profile of v1, /device:TPU:0, one launch (start us, length us, event | category | flops | bytes accessed | tf_op | source)
XLA Modules:
  0.0 88.7 jit_solution(18345907856382566244)
XLA Ops:
  0.0 0.0 copy-start
  0.0 1.4 %copy.9.routes = s32[128,6]{1,0:T(8,128)} copy(s32[128,6]{0,1:T(8,128)} %param.11) | data formatting | bytes 6144 | tf_op args[4]
  1.4 0.0 copy-done
  1.4 0.7 copy.10.scores
  2.2 2.5 %copy.8.down = f32[2,512,192]{2,1,0:T(8,128)} copy(f32[2,512,192]{1,2,0:T(8,128)} %param.10) | data formatting | bytes 1572864 | tf_op args[3]
  4.6 82.3 %shard_map.73 = bf16[128,1536]{1,0:T(8,128)(2,1)} custom-call(bf16[128,1536]{1,0:T(8,128)(2,1)} %tokens.1, f32[2,192,512]{2,1,0:T(8,128)} %gate.1, f32[2,192,512]{2,1,0:T(8,128)} %up.1, f32[2,512,192]{2,1,0:T(8,128)} %copy.8.down, s32[128,6]{1,0:T(8,128)} %copy.9.routes, f32[128,6]{1,0:T(8,128)} %copy.10.scores, s32[1,128]{1,0:T(1,128)} %bitcast.1), custom_call_target="tpu_custom_call" | custom-call | tf_op jit(solution)/shard_map/pallas_call | solution.py:290
  86.9 1.8 %copy.12 = bf16[128,1536]{1,0:T(8,128)(2,1)} copy(bf16[128,1536]{1,0:T(8,128)(2,1)} %shard_map.73) | data formatting | bytes 786432
Async XLA Ops:
  0.0 1.4 %copy-start = (f32[128,6]{0,1:T(8,128)S(1)}, f32[128,6]{0,1:T(8,128)}, u32[]{:S(2)}) copy-start(f32[128,6]{0,1:T(8,128)} %param.12) | copy-start | bytes 9220

commit v2 on v1

--- a/solution.py
+++ b/solution.py
@@ -24,13 +24,13 @@
 def kernel(
     n_group, n_hold, capacity,
     tokens, gate, up, down, routes, scores, live, out,
-    w_gu, w_down, tok_all, share_out, share_in, hidden, stage, back, flip, down_flip,
+    w_gu, w_down, tok_all, share_out, share_in, hidden, stage, back, flip, relay, ahead,
     gu_send, gu_recv, down_send, down_recv, tok_send, tok_recv, share_send, share_recv,
-    ret_send, ret_recv,
+    ret_send, ret_recv, relay_send, relay_recv,
 ):
     local, rows, ff = gate.shape
     block, width = tokens.shape
-    top = routes.shape[1]
+    top = routes.shape[0]
     experts = local * n_hold
     chips = n_group // 2
     square = chips == 4
@@ -41,6 +41,11 @@
     def device(group, expert):
         return (group, expert)
 
+    line = n_hold == 4
+    order = (0, 2, 1, 3) if line else tuple(range(n_hold))
+    at_low, at_high = holder == 0, holder == n_hold - 1
+    inner = jnp.logical_not(jnp.logical_or(at_low, at_high))
+
     def peer(d):
         return lax.rem(holder + d, n_hold)
 
@@ -55,20 +60,26 @@
         pl.semaphore_signal(barrier, inc=1, device_id=partner, device_id_type=MESH)
 
     mine = pl.multiple_of(me * rows, rows)
-    for e in range(local):
+
+    def round_gate_up(e):
         w_gu[e, pl.ds(mine, rows), :ff] = gate[e].astype(BF16)
         w_gu[e, pl.ds(mine, rows), ff:] = up[e].astype(BF16)
+
+    round_gate_up(0)
     pl.semaphore_wait(barrier, len(partners))
 
     started = []
 
-    def start(src, dst, send, recv, target):
+    def start(src, dst, send, recv, target, when=None):
         copy = pltpu.make_async_remote_copy(
             src_ref=src, dst_ref=dst, send_sem=send, recv_sem=recv,
             device_id=target, device_id_type=MESH,
         )
-        copy.start()
-        started.append(copy)
+        started.append((copy, when))
+        if when is None:
+            copy.start()
+        else:
+            pl.when(when)(copy.start)
 
     halves = 2 if square else 1
     half_rows = rows // halves
@@ -100,8 +111,7 @@
 
     def send_own(kind, keys):
         for key in keys:
-            order = near if key[-1] == 0 else near[::-1]
-            for j in order:
+            for j in near if key[-1] == 0 else near[::-1]:
                 send_piece(kind, key, me, j, xor(me, 2 * j))
         for key in keys:
             send_piece(kind, key, me, chips, sibling)
@@ -130,17 +140,17 @@
     down_keys = [(a,) for a in range(halves)]
 
     send_own("gu", gu_keys[0])
-    for d in range(1, n_hold):
-        start(tokens, tok_all.at[d], tok_send.at[d], tok_recv.at[d], device(me, peer(d)))
+    for i in range(1, n_hold):
+        d, when = order[i], None
+        if line and d != 2:
+            when = jnp.logical_not(at_high if d == 1 else at_low)
+        start(tokens, tok_all.at[i], tok_send.at[i], tok_recv.at[i], device(me, peer(d)), when)
     for e in range(1, local):
+        round_gate_up(e)
         send_own("gu", gu_keys[e])
 
-    flip[...] = jnp.zeros_like(flip)
-    flip[:, :top] = routes[...].astype(F32)
-    flip[:, 8:8 + top] = scores[...]
-    turned = flip[...].T
-    named_expert = turned[:top]
-    chosen = turned[8:8 + top]
+    named_expert = routes[...].astype(F32)
+    chosen = scores[...]
     chosen = chosen / jnp.sum(chosen, axis=0, keepdims=True)
     expert_id = lax.broadcasted_iota(jnp.int32, (experts, block), 0).astype(F32)
     weight = jnp.zeros((experts, block), F32)
@@ -160,22 +170,41 @@
     share_out[...] = jnp.zeros_like(share_out)
     for p in range(n_hold):
         share_out[p, :local, :] = weight[p * local:(p + 1) * local]
-    for d in range(1, n_hold):
+    for i in range(1, n_hold):
         start(
-            share_out.at[peer(d)], share_in.at[d], share_send.at[d], share_recv.at[d],
-            device(me, peer(d)),
+            share_out.at[peer(order[i])], share_in.at[i], share_send.at[i], share_recv.at[i],
+            device(me, peer(order[i])),
         )
 
     for e in range(local):
-        down_flip[:, :rows] = down[e]
-        w_down[pl.ds(mine, rows), e * ff:(e + 1) * ff] = (
-            down_flip[...].T[:rows].astype(BF16)
-        )
+        w_down[pl.ds(mine, rows), e * ff:(e + 1) * ff] = down[e].astype(BF16)
     tok_all[0] = tokens[...]
     share_in[0] = share_out[holder]
+    flip[...] = jnp.zeros_like(flip)
+    if line:
+        @pl.when(at_high)
+        def _():
+            back[order.index(1)] = jnp.zeros(back.shape[1:], BF16)
+
+        @pl.when(at_low)
+        def _():
+            back[order.index(3)] = jnp.zeros(back.shape[1:], BF16)
+
+    def arrive(dst, recv):
+        pltpu.make_async_remote_copy(
+            src_ref=dst, dst_ref=dst, send_sem=recv, recv_sem=recv,
+            device_id=device(sibling, holder), device_id_type=MESH,
+        ).wait_recv()
 
     for e in range(local):
         service_near("gu", gu_keys[e])
+        if line and e == 0:
+            pl.when(inner)(lambda: arrive(tok_all.at[1], tok_recv.at[1]))
+            slot = jnp.where(holder == 2, 3, 2)
+            start(
+                tok_all.at[1], tok_all.at[slot], tok_send.at[0], tok_recv.at[slot],
+                device(me, jnp.where(holder == 2, 3, 0)), inner,
+            )
         if e > 0:
             service_far("gu", gu_keys[e - 1])
     send_own("down", down_keys)
@@ -187,15 +216,12 @@
     tile = 256
     per_group = 2
 
-    def wait_tokens(d):
-        for src, dst, send, recv in (
-            (tokens, tok_all.at[d], tok_send.at[d], tok_recv.at[d]),
-            (share_out.at[0], share_in.at[d], share_send.at[d], share_recv.at[d]),
-        ):
-            pltpu.make_async_remote_copy(
-                src_ref=src, dst_ref=dst, send_sem=send, recv_sem=recv,
-                device_id=device(sibling, holder), device_id_type=MESH,
-            ).wait_recv()
+    def wait_tokens(i):
+        if line and i == 1:
+            pl.when(jnp.logical_not(inner))(lambda: arrive(tok_all.at[1], tok_recv.at[1]))
+        else:
+            arrive(tok_all.at[i], tok_recv.at[i])
+        arrive(share_in.at[i], share_recv.at[i])
 
     def hidden_group(first):
         count = per_group * block
@@ -236,6 +262,20 @@
             return 0
         return pl.multiple_of(xor(chip, part) * piece_width, piece_width)
 
+    def send_back(i, part, when=None):
+        start(
+            stage.at[i, part], back.at[i, part],
+            ret_send.at[i, part], ret_recv.at[i, part],
+            device(me, origin(order[i])), when,
+        )
+
+    def pass_on(part):
+        @pl.when(inner)
+        def _():
+            arrive(relay.at[part], relay_recv.at[part])
+            stage[1, part] = (ahead[part % 2] + relay[part].astype(F32)).astype(BF16)
+        send_back(1, part, inner)
+
     for part in range(parts):
         if parts == 1:
             service_far("down", down_keys)
@@ -255,36 +295,53 @@
             stage[first:first + count, part] = value.astype(BF16).reshape(
                 count, block, piece_width
             )
-        for d in range(n_hold - 1, 0, -1):
+            if line:
+                ahead[part % 2] = value[block:2 * block]
+        if line:
+            far = jnp.where(at_low, 2, 3)
             start(
-                stage.at[d, part], back.at[d, part], ret_send.at[d, part], ret_recv.at[d, part],
-                device(me, origin(d)),
-            )
+                stage.at[far, part], relay.at[part], relay_send.at[part], relay_recv.at[part],
+                device(me, jnp.where(at_low, 1, 2)), jnp.logical_not(inner),
+            )
+            send_back(1, part, jnp.logical_not(inner))
+            send_back(2, part, jnp.logical_not(at_low))
+            send_back(3, part, jnp.logical_not(at_high))
+            if part > 0:
+                pass_on(part - 1)
+            if part == parts - 1:
+                pass_on(part)
+        else:
+            for i in range(n_hold - 1, 0, -1):
+                send_back(i, part)
 
     for part in range(parts):
         total = stage[0, part].astype(F32)
-        for d in range(1, n_hold):
-            pltpu.make_async_remote_copy(
-                src_ref=stage.at[d, part], dst_ref=back.at[d, part],
-                send_sem=ret_send.at[d, part], recv_sem=ret_recv.at[d, part],
-                device_id=device(sibling, holder), device_id_type=MESH,
-            ).wait_recv()
-            total = total + back[d, part].astype(F32)
+        for i in range(1, n_hold):
+            def landed(i=i, part=part):
+                arrive(back.at[i, part], ret_recv.at[i, part])
+            if line and i > 1:
+                pl.when(jnp.logical_not(at_high if order[i] == 1 else at_low))(landed)
+            else:
+                landed()
+            total = total + back[i, part].astype(F32)
         out[:, pl.ds(column(part), piece_width)] = total.astype(BF16)
 
-    for copy in started:
-        copy.wait_send()
+    for copy, when in started:
+        if when is None:
+            copy.wait_send()
+        else:
+            pl.when(when)(copy.wait_send)
 
 
 def local(n_group, n_hold, tokens, gate, up, down, routes, scores, live):
     experts_here, rows, ff = gate.shape
     block, width = tokens.shape
-    top = routes.shape[1]
+    down, routes, scores = jnp.swapaxes(down, 1, 2), routes.T, scores.T
+    top = routes.shape[0]
     capacity = block * top // (experts_here * n_hold)
     chips = n_group // 2
     halves = 2 if chips == 4 else 1
     parts = chips if (2 * rows) % 128 == 0 else 1
-    padded = -(-rows // 128) * 128
     dma = pltpu.SemaphoreType.DMA
     vmem = pl.BlockSpec(memory_space=pltpu.VMEM)
     return pl.pallas_call(
@@ -302,7 +359,8 @@
             pltpu.VMEM((n_hold, parts, block, width // parts), BF16),
             pltpu.VMEM((n_hold, parts, block, width // parts), BF16),
             pltpu.VMEM((128, 128), F32),
-            pltpu.VMEM((ff, padded), F32),
+            pltpu.VMEM((parts, block, width // parts), BF16),
+            pltpu.VMEM((2, block, width // parts), F32),
             dma((experts_here * halves, 2 * chips)),
             dma((experts_here * halves, 2 * chips)),
             dma((halves, 2 * chips)),
@@ -313,6 +371,8 @@
             dma((n_hold,)),
             dma((n_hold, parts)),
             dma((n_hold, parts)),
+            dma((parts,)),
+            dma((parts,)),
         ],
         compiler_params=pltpu.CompilerParams(
             collective_id=0, has_side_effects=True, vmem_limit_bytes=56 * 2**20

time: 88.9 us -> 77.8 us (0.88)
  Pallas kernels: 82.3 us -> 75.9 us
  local copies, waits for them, and re-layouts: 6.39 us -> 1.77 us
    pallas_call x1, Pallas kernels: 82.3 us -> 75.9 us  [local(): pl.pallas_call(functools.partial(kernel, n_group, n_hold, capacity), out_...]
    unnamed x6 -> x1, local copies, waits for them, and re-layouts: 6.39 us -> 1.77 us
where the time goes in v2:
time: 77.8 us; the launch traced here: 77.6 us
  Pallas kernels  75.9 us (98%)
  local copies, waits for them, and re-layouts  1.77 us (2%)
    pallas_call x1, Pallas kernels, local(): pl.pallas_call(functools.partial(kernel, n_group, n_hold, capacity), out_...  75.9 us
    unnamed x1, local copies, waits for them, and re-layouts  1.77 us

profile of v2, /device:TPU:0, one launch (start us, length us, event | category | flops | bytes accessed | tf_op | source)
XLA Modules:
  0.0 77.6 jit_solution(11746507919657515486)
XLA Ops:
  0.0 75.9 %shard_map.73 = bf16[128,1536]{1,0:T(8,128)(2,1)} custom-call(bf16[128,1536]{1,0:T(8,128)(2,1)} %tokens.1, f32[2,192,512]{2,1,0:T(8,128)} %gate.1, f32[2,192,512]{2,1,0:T(8,128)} %up.1, f32[2,192,512]{2,1,0:T(8,128)} %bitcast.4, s32[6,128]{1,0:T(8,128)} %bitcast.5, f32[6,128]{1,0:T(8,128)} %bitcast.6, s32[1,128]{1,0:T(1,128)} %bitcast.7), custom_call_target="tpu_custom_call" | custom-call | tf_op jit(solution)/shard_map/pallas_call | solution.py:347
  75.9 1.8 %copy.9 = bf16[128,1536]{1,0:T(8,128)(2,1)} copy(bf16[128,1536]{1,0:T(8,128)(2,1)} %shard_map.73) | data formatting | bytes 786432

commit v3 on v2

--- a/solution.py
+++ b/solution.py
@@ -23,13 +23,13 @@
 
 def kernel(
     n_group, n_hold, capacity,
-    tokens, gate, up, down, routes, scores, live, out,
-    w_gu, w_down, tok_all, share_out, share_in, hidden, stage, back, flip, relay, ahead,
+    tokens_in, gate_in, up_in, down_in, routes, scores, live, out,
+    gate, up, down, load, w_gu, w_down, tok_all, share_out, share_in, hidden, stage, back, flip, relay, ahead,
     gu_send, gu_recv, down_send, down_recv, tok_send, tok_recv, share_send, share_recv,
-    ret_send, ret_recv, relay_send, relay_recv,
+    ret_send, ret_recv, relay_send, relay_recv, hand_send, hand_recv,
 ):
     local, rows, ff = gate.shape
-    block, width = tokens.shape
+    block, width = tokens_in.shape
     top = routes.shape[0]
     experts = local * n_hold
     chips = n_group // 2
@@ -56,12 +56,25 @@
     barrier = pltpu.get_barrier_semaphore()
     partners = [device(xor(me, 2 * j), holder) for j in near] + [device(sibling, holder)]
     partners += [device(me, peer(d)) for d in range(1, n_hold)]
+    loads = {}
+    tokens = tok_all.at[0]
+    for number, (name, src, dst) in enumerate(
+        [("gate0", gate_in.at[0], gate.at[0]), ("up0", up_in.at[0], up.at[0])]
+        + [("tokens", tokens_in, tokens)]
+        + [(name + str(e), src.at[e], dst.at[e]) for e in range(1, local) for name, src, dst in
+           (("gate", gate_in, gate), ("up", up_in, up))]
+        + [("down", down_in, down)]
+    ):
+        loads[name] = pltpu.make_async_copy(src, dst, load.at[number])
+        loads[name].start()
     for partner in partners:
         pl.semaphore_signal(barrier, inc=1, device_id=partner, device_id_type=MESH)
 
     mine = pl.multiple_of(me * rows, rows)
 
     def round_gate_up(e):
+        loads["gate" + str(e)].wait()
+        loads["up" + str(e)].wait()
         w_gu[e, pl.ds(mine, rows), :ff] = gate[e].astype(BF16)
         w_gu[e, pl.ds(mine, rows), ff:] = up[e].astype(BF16)
 
@@ -109,21 +122,26 @@
             device_id=device(sibling, holder), device_id_type=MESH,
         ).wait_recv()
 
-    def send_own(kind, keys):
-        for key in keys:
-            for j in near if key[-1] == 0 else near[::-1]:
-                send_piece(kind, key, me, j, xor(me, 2 * j))
+    def turns(keys):
+        if not square:
+            return [(key, j) for key in keys for j in near]
+        return [(keys[0], 1), (keys[1], 2), (keys[1], 1), (keys[0], 2)]
+
+    def send_own(kind, some):
+        for key, j in some:
+            send_piece(kind, key, me, j, xor(me, 2 * j))
+
+    def send_core(kind, keys):
         for key in keys:
             send_piece(kind, key, me, chips, sibling)
 
-    def service_near(kind, keys):
-        for key in keys:
-            for j in near:
-                owner = xor(me, 2 * j)
-                wait_piece(kind, key, owner, j)
-                if square and (j == 1) == (key[-1] == 0):
-                    send_piece(kind, key, owner, 3, xor(me, 2 * (3 - j)))
-                send_piece(kind, key, owner, chips + j, sibling)
+    def service_near(kind, some):
+        for key, j in some:
+            owner = xor(me, 2 * j)
+            wait_piece(kind, key, owner, j)
+            if square and (j == 1) == (key[-1] == 0):
+                send_piece(kind, key, owner, 3, xor(me, 2 * (3 - j)))
+            send_piece(kind, key, owner, chips + j, sibling)
 
     def service_far(kind, keys):
         if square:
@@ -139,15 +157,32 @@
     gu_keys = [[(e, a) for a in range(halves)] for e in range(local)]
     down_keys = [(a,) for a in range(halves)]
 
-    send_own("gu", gu_keys[0])
-    for i in range(1, n_hold):
+    def half_block(i, half):
+        return tok_all.at[i, pl.ds(half * (block // 2), block // 2), :]
+
+    def send_tokens(i):
         d, when = order[i], None
         if line and d != 2:
             when = jnp.logical_not(at_high if d == 1 else at_low)
         start(tokens, tok_all.at[i], tok_send.at[i], tok_recv.at[i], device(me, peer(d)), when)
+
+    first_turns = turns(gu_keys[0])
+    send_own("gu", first_turns[:2])
+    loads["tokens"].wait()
+    if line:
+        for half in range(2):
+            start(
+                half_block(0, half), half_block(1, half), hand_send.at[half], hand_recv.at[half],
+                device(me, peer(2)),
+            )
+    send_own("gu", first_turns[2:])
+    for i in range(2 if line else 1, n_hold):
+        send_tokens(i)
     for e in range(1, local):
         round_gate_up(e)
-        send_own("gu", gu_keys[e])
+        send_own("gu", turns(gu_keys[e]))
+    for e in range(local):
+        send_core("gu", gu_keys[e])
 
     named_expert = routes[...].astype(F32)
     chosen = scores[...]
@@ -176,9 +211,9 @@
             device(me, peer(order[i])),
         )
 
+    loads["down"].wait()
     for e in range(local):
         w_down[pl.ds(mine, rows), e * ff:(e + 1) * ff] = down[e].astype(BF16)
-    tok_all[0] = tokens[...]
     share_in[0] = share_out[holder]
     flip[...] = jnp.zeros_like(flip)
     if line:
@@ -196,64 +231,86 @@
             device_id=device(sibling, holder), device_id_type=MESH,
         ).wait_recv()
 
+    far_slot = jnp.where(holder == 2, 3, 2)
+    far_end = jnp.where(holder == 2, 3, 0)
+
+    def hand_on(half):
+        if line:
+            arrive(half_block(1, half), hand_recv.at[half])
+            start(
+                half_block(1, half), half_block(far_slot, half),
+                hand_send.at[2 + half], hand_recv.at[2 + half], device(me, far_end), inner,
+            )
+
     for e in range(local):
-        service_near("gu", gu_keys[e])
-        if line and e == 0:
-            pl.when(inner)(lambda: arrive(tok_all.at[1], tok_recv.at[1]))
-            slot = jnp.where(holder == 2, 3, 2)
-            start(
-                tok_all.at[1], tok_all.at[slot], tok_send.at[0], tok_recv.at[slot],
-                device(me, jnp.where(holder == 2, 3, 0)), inner,
-            )
-        if e > 0:
-            service_far("gu", gu_keys[e - 1])
-    send_own("down", down_keys)
-    service_far("gu", gu_keys[local - 1])
-    for e in range(local):
-        for j in range(chips):
-            wait_sibling("gu", gu_keys[e], j)
+        some = turns(gu_keys[e])
+        if e == 0:
+            service_near("gu", some)
+            hand_on(0)
+        elif e == 1:
+            service_near("gu", some[:2])
+            hand_on(1)
+            service_near("gu", some[2:])
+        else:
+            service_near("gu", some)
+        if e < local - 1:
+            service_far("gu", gu_keys[e])
+    send_own("down", turns(down_keys))
+    send_core("down", down_keys)
 
     tile = 256
     per_group = 2
 
     def wait_tokens(i):
-        if line and i == 1:
-            pl.when(jnp.logical_not(inner))(lambda: arrive(tok_all.at[1], tok_recv.at[1]))
-        else:
+        if line and i > 1:
+            from_end = at_high if order[i] == 3 else at_low
+
+            @pl.when(from_end)
+            def _():
+                for half in range(2):
+                    arrive(half_block(i, half), hand_recv.at[2 + half])
+
+            pl.when(jnp.logical_not(from_end))(lambda: arrive(tok_all.at[i], tok_recv.at[i]))
+        elif not line:
             arrive(tok_all.at[i], tok_recv.at[i])
         arrive(share_in.at[i], share_recv.at[i])
 
-    def hidden_group(first):
+    def hidden_group(first, e):
         count = per_group * block
         flip[: per_group * 8] = share_in[first:first + per_group].reshape(per_group * 8, block)
         columns = flip[...].T
         picked = tok_all[first:first + per_group].reshape(count, width)
+        scale = jnp.concatenate(
+            [columns[:, i * 8 + e:i * 8 + e + 1] for i in range(per_group)], axis=0
+        )
+
+        def body(j, carry):
+            at = pl.multiple_of(j * tile, tile)
+            g = jnp.dot(picked, w_gu[e, :, pl.ds(at, tile)], preferred_element_type=F32)
+            u = jnp.dot(
+                picked, w_gu[e, :, pl.ds(pl.multiple_of(ff + at, tile), tile)],
+                preferred_element_type=F32,
+            )
+            value = (g / (1.0 + jnp.exp(-g))) * u * scale
+            hidden[first * block:first * block + count,
+                   pl.ds(pl.multiple_of(e * ff + at, tile), tile)] = value.astype(BF16)
+            return carry
+
+        lax.fori_loop(0, ff // tile, body, 0)
+
+    wait_tokens(1)
+    for e in range(local):
+        if e == local - 1:
+            service_far("gu", gu_keys[e])
+        for j in range(chips):
+            wait_sibling("gu", gu_keys[e], j)
+        hidden_group(0, e)
+    service_near("down", turns(down_keys))
+    for first in range(per_group, n_hold, per_group):
+        for i in range(first, first + per_group):
+            wait_tokens(i)
         for e in range(local):
-            scale = jnp.concatenate(
-                [columns[:, i * 8 + e:i * 8 + e + 1] for i in range(per_group)], axis=0
-            )
-
-            def body(j, carry):
-                at = pl.multiple_of(j * tile, tile)
-                g = jnp.dot(picked, w_gu[e, :, pl.ds(at, tile)], preferred_element_type=F32)
-                u = jnp.dot(
-                    picked, w_gu[e, :, pl.ds(pl.multiple_of(ff + at, tile), tile)],
-                    preferred_element_type=F32,
-                )
-                value = (g / (1.0 + jnp.exp(-g))) * u * scale
-                hidden[first * block:first * block + count,
-                       pl.ds(pl.multiple_of(e * ff + at, tile), tile)] = value.astype(BF16)
-                return carry
-
-            lax.fori_loop(0, ff // tile, body, 0)
-
-    for first in range(0, n_hold, per_group):
-        if first == per_group or n_hold == per_group:
-            service_near("down", down_keys)
-        for d in range(first, first + per_group):
-            if d > 0:
-                wait_tokens(d)
-        hidden_group(first)
+            hidden_group(first, e)
 
     parts, piece_width = back.shape[1], back.shape[3]
 
@@ -347,9 +404,13 @@
     return pl.pallas_call(
         functools.partial(kernel, n_group, n_hold, capacity),
         out_shape=jax.ShapeDtypeStruct((block, width), BF16),
-        in_specs=[vmem] * 7,
+        in_specs=[pl.BlockSpec(memory_space=pl.ANY)] * 4 + [vmem] * 3,
         out_specs=vmem,
         scratch_shapes=[
+            pltpu.VMEM(gate.shape, F32),
+            pltpu.VMEM(up.shape, F32),
+            pltpu.VMEM(down.shape, F32),
+            dma((2 + 2 * experts_here,)),
             pltpu.VMEM((experts_here, width, 2 * ff), BF16),
             pltpu.VMEM((width, experts_here * ff), BF16),
             pltpu.VMEM((n_hold, block, width), BF16),
@@ -373,6 +434,8 @@
             dma((n_hold, parts)),
             dma((parts,)),
             dma((parts,)),
+            dma((4,)),
+            dma((4,)),
         ],
         compiler_params=pltpu.CompilerParams(
             collective_id=0, has_side_effects=True, vmem_limit_bytes=56 * 2**20

time: 77.8 us -> 78.4 us (level)
  no operation moved by 1% of the time
where the time goes in v3:
time: 78.4 us; the launch traced here: 78.2 us
  Pallas kernels  76.4 us (97%)
  local copies, waits for them, and re-layouts  1.77 us (2%)
    pallas_call x1, Pallas kernels, local(): pl.pallas_call(functools.partial(kernel, n_group, n_hold, capacity), out_...  76.4 us
    unnamed x1, local copies, waits for them, and re-layouts  1.77 us

profile of v3, /device:TPU:0, one launch (start us, length us, event | category | flops | bytes accessed | tf_op | source)
XLA Modules:
  0.0 78.2 jit_solution(7441078262538664945)
XLA Ops:
  0.0 76.4 %shard_map.73 = bf16[128,1536]{1,0:T(8,128)(2,1)} custom-call(bf16[128,1536]{1,0:T(8,128)(2,1)} %tokens_in.1, f32[2,192,512]{2,1,0:T(8,128)} %gate_in.1, f32[2,192,512]{2,1,0:T(8,128)} %up_in.1, f32[2,192,512]{2,1,0:T(8,128)} %bitcast.4, s32[6,128]{1,0:T(8,128)} %bitcast.5, f32[6,128]{1,0:T(8,128)} %bitcast.6, s32[1,128]{1,0:T(1,128)} %bitcast.7), custom_call_target="tpu_custom_call" | custom-call | tf_op jit(solution)/shard_map/pallas_call | solution.py:404
  76.4 1.8 %copy.9 = bf16[128,1536]{1,0:T(8,128)(2,1)} copy(bf16[128,1536]{1,0:T(8,128)(2,1)} %shard_map.73) | data formatting | bytes 786432

commit v4 on v3

--- a/solution.py
+++ b/solution.py
@@ -41,7 +41,7 @@
     def device(group, expert):
         return (group, expert)
 
-    line = n_hold == 4
+    line = n_hold == 4 and square and rows % 64 == 0
     order = (0, 2, 1, 3) if line else tuple(range(n_hold))
     at_low, at_high = holder == 0, holder == n_hold - 1
     inner = jnp.logical_not(jnp.logical_or(at_low, at_high))
@@ -298,20 +298,6 @@
 
         lax.fori_loop(0, ff // tile, body, 0)
 
-    wait_tokens(1)
-    for e in range(local):
-        if e == local - 1:
-            service_far("gu", gu_keys[e])
-        for j in range(chips):
-            wait_sibling("gu", gu_keys[e], j)
-        hidden_group(0, e)
-    service_near("down", turns(down_keys))
-    for first in range(per_group, n_hold, per_group):
-        for i in range(first, first + per_group):
-            wait_tokens(i)
-        for e in range(local):
-            hidden_group(first, e)
-
     parts, piece_width = back.shape[1], back.shape[3]
 
     def column(part):
@@ -333,43 +319,87 @@
             stage[1, part] = (ahead[part % 2] + relay[part].astype(F32)).astype(BF16)
         send_back(1, part, inner)
 
-    for part in range(parts):
-        if parts == 1:
-            service_far("down", down_keys)
+    def rows_out(part, first, count):
+        at = column(part)
+        value = lax.dot_general(
+            hidden[first * block:(first + count) * block, :],
+            w_down[pl.ds(at, piece_width), :], PAIR, preferred_element_type=F32,
+        )
+        stage[first:first + count, part] = value.astype(BF16).reshape(count, block, piece_width)
+        if line and first == 0:
+            ahead[part % 2] = value[block:2 * block]
+
+    def send_relay(part):
+        far = jnp.where(at_low, 2, 3)
+        start(
+            stage.at[far, part], relay.at[part], relay_send.at[part], relay_recv.at[part],
+            device(me, jnp.where(at_low, 1, 2)), jnp.logical_not(inner),
+        )
+
+    def send_near(part):
+        send_back(2, part, jnp.logical_not(at_low))
+        send_back(3, part, jnp.logical_not(at_high))
+
+    if line:
+        wait_tokens(1)
+        for e in range(local):
+            last = e == local - 1
+            if last:
+                service_far("gu", gu_keys[e])
             for j in range(chips):
-                wait_sibling("down", down_keys, j)
-        else:
-            if part == min(2, parts - 1):
+                if not last:
+                    wait_sibling("gu", gu_keys[e], j)
+            if not last:
+                hidden_group(0, e)
+        for i in range(2, n_hold):
+            wait_tokens(i)
+        for e in range(local - 1):
+            hidden_group(2, e)
+        for j in range(chips):
+            wait_sibling("gu", gu_keys[local - 1], j)
+        hidden_group(0, local - 1)
+        wait_sibling("down", down_keys, 0)
+        rows_out(0, 0, 2)
+        send_back(1, 0, jnp.logical_not(inner))
+        hidden_group(2, local - 1)
+        rows_out(0, 2, 2)
+        send_relay(0)
+        send_near(0)
+        down_turns = turns(down_keys)
+        service_near("down", down_turns[:2])
+        pass_on(0)
+        service_near("down", down_turns[2:])
+        for part in range(1, parts):
+            if part == parts - 1:
                 service_far("down", down_keys)
             wait_sibling("down", down_keys, part)
-        at = column(part)
-        for first in range(0, n_hold, 4):
-            count = min(4, n_hold - first)
-            value = lax.dot_general(
-                hidden[first * block:(first + count) * block, :],
-                w_down[pl.ds(at, piece_width), :], PAIR, preferred_element_type=F32,
-            )
-            stage[first:first + count, part] = value.astype(BF16).reshape(
-                count, block, piece_width
-            )
-            if line:
-                ahead[part % 2] = value[block:2 * block]
-        if line:
-            far = jnp.where(at_low, 2, 3)
-            start(
-                stage.at[far, part], relay.at[part], relay_send.at[part], relay_recv.at[part],
-                device(me, jnp.where(at_low, 1, 2)), jnp.logical_not(inner),
-            )
+            rows_out(part, 0, n_hold)
+            send_relay(part)
             send_back(1, part, jnp.logical_not(inner))
-            send_back(2, part, jnp.logical_not(at_low))
-            send_back(3, part, jnp.logical_not(at_high))
-            if part > 0:
+            send_near(part)
+            if part > 1:
                 pass_on(part - 1)
-            if part == parts - 1:
-                pass_on(part)
-        else:
-            for i in range(n_hold - 1, 0, -1):
-                send_back(i, part)
+        pass_on(parts - 1)
+    else:
+        for e in range(local):
+            if e == local - 1:
+                service_far("gu", gu_keys[e])
+            for j in range(chips):
+                wait_sibling("gu", gu_keys[e], j)
+        service_near("down", turns(down_keys))
+        service_far("down", down_keys)
+        for j in range(chips):
+            wait_sibling("down", down_keys, j)
+        for i in range(1, n_hold):
+            wait_tokens(i)
+        for first in range(0, n_hold, per_group):
+            for e in range(local):
+                hidden_group(first, e)
+            for part in range(parts):
+                rows_out(part, first, per_group)
+                for i in range(first, first + per_group):
+                    if i > 0:
+                        send_back(i, part)
 
     for part in range(parts):
         total = stage[0, part].astype(F32)

time: 78.4 us -> 73.1 us (0.932)
  Pallas kernels: 76.4 us -> 71.1 us
    pallas_call x1, Pallas kernels: 76.4 us -> 71.1 us  [local(): pl.pallas_call(functools.partial(kernel, n_group, n_hold, capacity), out_...]
where the time goes in v4:
time: 73.1 us; the launch traced here: 72.9 us
  Pallas kernels  71.1 us (97%)
  local copies, waits for them, and re-layouts  1.77 us (2%)
    pallas_call x1, Pallas kernels, local(): pl.pallas_call(functools.partial(kernel, n_group, n_hold, capacity), out_...  71.1 us
    unnamed x1, local copies, waits for them, and re-layouts  1.77 us

profile of v4, /device:TPU:0, one launch (start us, length us, event | category | flops | bytes accessed | tf_op | source)
XLA Modules:
  0.0 72.9 jit_solution(13405040467288161662)
XLA Ops:
  0.0 71.1 %shard_map.73 = bf16[128,1536]{1,0:T(8,128)(2,1)} custom-call(bf16[128,1536]{1,0:T(8,128)(2,1)} %tokens_in.1, f32[2,192,512]{2,1,0:T(8,128)} %gate_in.1, f32[2,192,512]{2,1,0:T(8,128)} %up_in.1, f32[2,192,512]{2,1,0:T(8,128)} %bitcast.4, s32[6,128]{1,0:T(8,128)} %bitcast.5, f32[6,128]{1,0:T(8,128)} %bitcast.6, s32[1,128]{1,0:T(1,128)} %bitcast.7), custom_call_target="tpu_custom_call" | custom-call | tf_op jit(solution)/shard_map/pallas_call | solution.py:434
  71.1 1.8 %copy.9 = bf16[128,1536]{1,0:T(8,128)(2,1)} copy(bf16[128,1536]{1,0:T(8,128)(2,1)} %shard_map.73) | data formatting | bytes 786432

commit v5 on v4

--- a/solution.py
+++ b/solution.py
@@ -255,7 +255,6 @@
             service_near("gu", some)
         if e < local - 1:
             service_far("gu", gu_keys[e])
-    send_own("down", turns(down_keys))
     send_core("down", down_keys)
 
     tile = 256
@@ -346,6 +345,7 @@
             last = e == local - 1
             if last:
                 service_far("gu", gu_keys[e])
+                send_own("down", turns(down_keys))
             for j in range(chips):
                 if not last:
                     wait_sibling("gu", gu_keys[e], j)
@@ -384,6 +384,7 @@
         for e in range(local):
             if e == local - 1:
                 service_far("gu", gu_keys[e])
+                send_own("down", turns(down_keys))
             for j in range(chips):
                 wait_sibling("gu", gu_keys[e], j)
         service_near("down", turns(down_keys))
@@ -433,7 +434,7 @@
     vmem = pl.BlockSpec(memory_space=pltpu.VMEM)
     return pl.pallas_call(
         functools.partial(kernel, n_group, n_hold, capacity),
-        out_shape=jax.ShapeDtypeStruct((block, width), BF16),
+        out_shape=pltpu.VMEM((block, width), BF16),
         in_specs=[pl.BlockSpec(memory_space=pl.ANY)] * 4 + [vmem] * 3,
         out_specs=vmem,
         scratch_shapes=[
@@ -468,7 +469,7 @@
             dma((4,)),
         ],
         compiler_params=pltpu.CompilerParams(
-            collective_id=0, has_side_effects=True, vmem_limit_bytes=56 * 2**20
+            collective_id=0, has_side_effects=True, vmem_limit_bytes=52 * 2**20
         ),
     )(tokens, gate, up, down, routes, scores, live.reshape(1, block))
 

time: 73.1 us -> 74.2 us (1.015)
  local copies, waits for them, and re-layouts: 1.77 us -> 4.25 us
  Pallas kernels: 71.1 us -> 69.7 us
    unnamed x1 -> x11, local copies, waits for them, and re-layouts: 1.77 us -> 4.25 us
    pallas_call x1, Pallas kernels: 71.1 us -> 69.7 us  [local(): pl.pallas_call(functools.partial(kernel, n_group, n_hold, capacity), out_...]
where the time goes in v5:
time: 74.2 us; the launch traced here: 74 us
  Pallas kernels  69.7 us (94%)
  local copies, waits for them, and re-layouts  4.25 us (6%)
    pallas_call x1, Pallas kernels, local(): pl.pallas_call(functools.partial(kernel, n_group, n_hold, capacity), out_...  69.7 us
    unnamed x11, local copies, waits for them, and re-layouts  4.25 us

profile of v5, /device:TPU:0, one launch (start us, length us, event | category | flops | bytes accessed | tf_op | source)
XLA Modules:
  0.0 74.0 jit_solution(8066720133377055708)
XLA Ops:
  0.0 0.0 copy-start.2
  0.0 0.0 copy-start.4
  0.0 0.7 copy-done.2
  0.7 0.0 copy-done.4
  0.7 0.0 copy-start
  0.7 1.1 %copy-done = f32[2,192,512]{2,1,0:T(8,128)S(1)} copy-done((f32[2,192,512]{2,1,0:T(8,128)S(1)}, f32[2,192,512]{2,1,0:T(8,128)}, u32[]{:S(2)}) %copy-start) | copy-done | bytes 786456
  1.8 0.0 copy-start.1
  1.8 1.0 %copy-done.1 = bf16[128,1536]{1,0:T(8,128)(2,1)S(1)} copy-done((bf16[128,1536]{1,0:T(8,128)(2,1)S(1)}, bf16[128,1536]{1,0:T(8,128)(2,1)}, u32[]{:S(2)}) %copy-start.1) | copy-done | bytes 393240
  2.8 0.0 copy-start.3
  2.8 0.7 copy-done.3
  3.5 69.7 %shard_map.73 = bf16[128,1536]{1,0:T(8,128)(2,1)S(1)} custom-call(bf16[128,1536]{1,0:T(8,128)(2,1)S(1)} %copy-done.1, f32[2,192,512]{2,1,0:T(8,128)S(1)} %copy-done, f32[2,192,512]{2,1,0:T(8,128)} %up_in.1, f32[2,192,512]{2,1,0:T(8,128)} %bitcast.7, s32[6,128]{1,0:T(8,128)S(1)} %bitcast.4, f32[6,128]{1,0:T(8,128)S(1)} %bitcast.5, s32[1,128]{1,0:T(1,128)S(1)} %bitcast.6), custom_call_target="tpu_custom_call" | custom-call | tf_op jit(solution)/shard_map/pallas_call | solution.py:435
  73.2 0.7 %copy.9 = bf16[128,1536]{1,0:T(8,128)(2,1)} copy(bf16[128,1536]{1,0:T(8,128)(2,1)S(1)} %shard_map.73) | data formatting | bytes 786432
Async XLA Ops:
  0.0 0.7 copy-start.2
  0.0 0.7 copy-start.4
  0.7 1.1 %copy-start = (f32[2,192,512]{2,1,0:T(8,128)S(1)}, f32[2,192,512]{2,1,0:T(8,128)}, u32[]{:S(2)}) copy-start(f32[2,192,512]{2,1,0:T(8,128)} %gate_in.1) | copy-start | bytes 2359300
  1.8 1.0 %copy-start.1 = (bf16[128,1536]{1,0:T(8,128)(2,1)S(1)}, bf16[128,1536]{1,0:T(8,128)(2,1)}, u32[]{:S(2)}) copy-start(bf16[128,1536]{1,0:T(8,128)(2,1)} %tokens_in.1) | copy-start | bytes 1179652
  2.8 0.7 copy-start.3

commit v6 on v5

--- a/solution.py
+++ b/solution.py
@@ -336,8 +336,12 @@
         )
 
     def send_near(part):
-        send_back(2, part, jnp.logical_not(at_low))
-        send_back(3, part, jnp.logical_not(at_high))
+        send_back(2, part, inner)
+        send_back(3, part, inner)
+
+    def send_near_end(part):
+        send_back(2, part, at_high)
+        send_back(3, part, at_low)
 
     if line:
         wait_tokens(1)
@@ -365,6 +369,7 @@
         rows_out(0, 2, 2)
         send_relay(0)
         send_near(0)
+        send_near_end(0)
         down_turns = turns(down_keys)
         service_near("down", down_turns[:2])
         pass_on(0)
@@ -377,6 +382,10 @@
             send_relay(part)
             send_back(1, part, jnp.logical_not(inner))
             send_near(part)
+            if part > 1:
+                send_near_end(part - 1)
+            if part == parts - 1:
+                send_near_end(part)
             if part > 1:
                 pass_on(part - 1)
         pass_on(parts - 1)
@@ -435,7 +444,7 @@
     return pl.pallas_call(
         functools.partial(kernel, n_group, n_hold, capacity),
         out_shape=pltpu.VMEM((block, width), BF16),
-        in_specs=[pl.BlockSpec(memory_space=pl.ANY)] * 4 + [vmem] * 3,
+        in_specs=[pl.BlockSpec(memory_space=pltpu.HBM)] * 4 + [vmem] * 3,
         out_specs=vmem,
         scratch_shapes=[
             pltpu.VMEM(gate.shape, F32),
@@ -469,7 +478,7 @@
             dma((4,)),
         ],
         compiler_params=pltpu.CompilerParams(
-            collective_id=0, has_side_effects=True, vmem_limit_bytes=52 * 2**20
+            collective_id=0, has_side_effects=True, vmem_limit_bytes=58 * 2**20
         ),
     )(tokens, gate, up, down, routes, scores, live.reshape(1, block))
 

time: 74.2 us -> 69.9 us (0.942)
  local copies, waits for them, and re-layouts: 4.25 us -> 0.75 us
    unnamed x11 -> x1, local copies, waits for them, and re-layouts: 4.25 us -> 0.75 us
where the time goes in v6:
time: 69.9 us; the launch traced here: 69.8 us
  Pallas kernels  69 us (99%)
  local copies, waits for them, and re-layouts  0.75 us (1%)
    pallas_call x1, Pallas kernels, local(): pl.pallas_call(functools.partial(kernel, n_group, n_hold, capacity), out_...  69 us

profile of v6, /device:TPU:0, one launch (start us, length us, event | category | flops | bytes accessed | tf_op | source)
XLA Modules:
  0.0 69.8 jit_solution(16460925425201716279)
XLA Ops:
  0.0 69.0 %shard_map.73 = bf16[128,1536]{1,0:T(8,128)(2,1)S(1)} custom-call(bf16[128,1536]{1,0:T(8,128)(2,1)} %tokens_in.1, f32[2,192,512]{2,1,0:T(8,128)} %gate_in.1, f32[2,192,512]{2,1,0:T(8,128)} %up_in.1, f32[2,192,512]{2,1,0:T(8,128)} %bitcast.4, s32[6,128]{1,0:T(8,128)} %bitcast.5, f32[6,128]{1,0:T(8,128)} %bitcast.6, s32[1,128]{1,0:T(1,128)} %bitcast.7), custom_call_target="tpu_custom_call" | custom-call | tf_op jit(solution)/shard_map/pallas_call | solution.py:444
  69.0 0.7 %copy.9 = bf16[128,1536]{1,0:T(8,128)(2,1)} copy(bf16[128,1536]{1,0:T(8,128)(2,1)S(1)} %shard_map.73) | data formatting | bytes 786432

commit v7 on v6

--- a/solution.py
+++ b/solution.py
@@ -23,8 +23,8 @@
 
 def kernel(
     n_group, n_hold, capacity,
-    tokens_in, gate_in, up_in, down_in, routes, scores, live, out,
-    gate, up, down, load, w_gu, w_down, tok_all, share_out, share_in, hidden, stage, back, flip, relay, ahead,
+    tokens_in, gate_in, up_in, down_in, routes_in, scores_in, live_in, out,
+    gate, up, down, routes, scores, live, load, w_gu, w_down, tok_all, share_out, share_in, hidden, stage, back, flip, relay, ahead,
     gu_send, gu_recv, down_send, down_recv, tok_send, tok_recv, share_send, share_recv,
     ret_send, ret_recv, relay_send, relay_recv, hand_send, hand_recv,
 ):
@@ -56,6 +56,8 @@
     barrier = pltpu.get_barrier_semaphore()
     partners = [device(xor(me, 2 * j), holder) for j in near] + [device(sibling, holder)]
     partners += [device(me, peer(d)) for d in range(1, n_hold)]
+    for partner in partners:
+        pl.semaphore_signal(barrier, inc=1, device_id=partner, device_id_type=MESH)
     loads = {}
     tokens = tok_all.at[0]
     for number, (name, src, dst) in enumerate(
@@ -63,12 +65,11 @@
         + [("tokens", tokens_in, tokens)]
         + [(name + str(e), src.at[e], dst.at[e]) for e in range(1, local) for name, src, dst in
            (("gate", gate_in, gate), ("up", up_in, up))]
+        + [("routes", routes_in, routes), ("scores", scores_in, scores), ("live", live_in, live)]
         + [("down", down_in, down)]
     ):
         loads[name] = pltpu.make_async_copy(src, dst, load.at[number])
         loads[name].start()
-    for partner in partners:
-        pl.semaphore_signal(barrier, inc=1, device_id=partner, device_id_type=MESH)
 
     mine = pl.multiple_of(me * rows, rows)
 
@@ -184,6 +185,8 @@
     for e in range(local):
         send_core("gu", gu_keys[e])
 
+    for name in ("routes", "scores", "live"):
+        loads[name].wait()
     named_expert = routes[...].astype(F32)
     chosen = scores[...]
     chosen = chosen / jnp.sum(chosen, axis=0, keepdims=True)
@@ -361,15 +364,15 @@
             hidden_group(2, e)
         for j in range(chips):
             wait_sibling("gu", gu_keys[local - 1], j)
-        hidden_group(0, local - 1)
+        hidden_group(2, local - 1)
         wait_sibling("down", down_keys, 0)
-        rows_out(0, 0, 2)
-        send_back(1, 0, jnp.logical_not(inner))
-        hidden_group(2, local - 1)
         rows_out(0, 2, 2)
         send_relay(0)
         send_near(0)
         send_near_end(0)
+        hidden_group(0, local - 1)
+        rows_out(0, 0, 2)
+        send_back(1, 0, jnp.logical_not(inner))
         down_turns = turns(down_keys)
         service_near("down", down_turns[:2])
         pass_on(0)
@@ -444,13 +447,16 @@
     return pl.pallas_call(
         functools.partial(kernel, n_group, n_hold, capacity),
         out_shape=pltpu.VMEM((block, width), BF16),
-        in_specs=[pl.BlockSpec(memory_space=pltpu.HBM)] * 4 + [vmem] * 3,
+        in_specs=[pl.BlockSpec(memory_space=pltpu.HBM)] * 7,
         out_specs=vmem,
         scratch_shapes=[
             pltpu.VMEM(gate.shape, F32),
             pltpu.VMEM(up.shape, F32),
             pltpu.VMEM(down.shape, F32),
-            dma((2 + 2 * experts_here,)),
+            pltpu.VMEM(routes.shape, jnp.int32),
+            pltpu.VMEM(scores.shape, F32),
+            pltpu.VMEM((1, block), jnp.int32),
+            dma((5 + 2 * experts_here,)),
             pltpu.VMEM((experts_here, width, 2 * ff), BF16),
             pltpu.VMEM((width, experts_here * ff), BF16),
             pltpu.VMEM((n_hold, block, width), BF16),

time: 69.9 us -> 69 us (0.987)
  Pallas kernels: 69 us -> 68.1 us
    pallas_call x1, Pallas kernels: 69 us -> 68.1 us  [local(): pl.pallas_call(functools.partial(kernel, n_group, n_hold, capacity), out_...]
where the time goes in v7:
time: 69 us; the launch traced here: 68.9 us
  Pallas kernels  68.1 us (99%)
  local copies, waits for them, and re-layouts  0.75 us (1%)
    pallas_call x1, Pallas kernels, local(): pl.pallas_call(functools.partial(kernel, n_group, n_hold, capacity), out_...  68.1 us

profile of v7, /device:TPU:0, one launch (start us, length us, event | category | flops | bytes accessed | tf_op | source)
XLA Modules:
  0.0 68.9 jit_solution(7768082191037603586)
XLA Ops:
  0.0 68.1 %shard_map.73 = bf16[128,1536]{1,0:T(8,128)(2,1)S(1)} custom-call(bf16[128,1536]{1,0:T(8,128)(2,1)} %tokens_in.1, f32[2,192,512]{2,1,0:T(8,128)} %gate_in.1, f32[2,192,512]{2,1,0:T(8,128)} %up_in.1, f32[2,192,512]{2,1,0:T(8,128)} %bitcast.4, s32[6,128]{1,0:T(8,128)} %bitcast.5, f32[6,128]{1,0:T(8,128)} %bitcast.6, s32[1,128]{1,0:T(1,128)} %bitcast.7), custom_call_target="tpu_custom_call" | custom-call | tf_op jit(solution)/shard_map/pallas_call | solution.py:447
  68.1 0.7 %copy.9 = bf16[128,1536]{1,0:T(8,128)(2,1)} copy(bf16[128,1536]{1,0:T(8,128)(2,1)S(1)} %shard_map.73) | data formatting | bytes 786432

commit v8 on v7

--- a/solution.py
+++ b/solution.py
@@ -24,7 +24,7 @@
 def kernel(
     n_group, n_hold, capacity,
     tokens_in, gate_in, up_in, down_in, routes_in, scores_in, live_in, out,
-    gate, up, down, routes, scores, live, load, w_gu, w_down, tok_all, share_out, share_in, hidden, stage, back, flip, relay, ahead,
+    gate, up, down, routes, scores, live, load, w_gu, w_down, tok_all, share_out, share_in, hidden, stage, back, flip, relay, ahead, early,
     gu_send, gu_recv, down_send, down_recv, tok_send, tok_recv, share_send, share_recv,
     ret_send, ret_recv, relay_send, relay_recv, hand_send, hand_recv,
 ):
@@ -248,12 +248,10 @@
     for e in range(local):
         some = turns(gu_keys[e])
         if e == 0:
-            service_near("gu", some)
+            service_near("gu", some[:2])
             hand_on(0)
-        elif e == 1:
-            service_near("gu", some[:2])
+            service_near("gu", some[2:])
             hand_on(1)
-            service_near("gu", some[2:])
         else:
             service_near("gu", some)
         if e < local - 1:
@@ -277,7 +275,27 @@
             arrive(tok_all.at[i], tok_recv.at[i])
         arrive(share_in.at[i], share_recv.at[i])
 
-    def hidden_group(first, e):
+    def chip_product(first, e, j, at):
+        base = pl.multiple_of(xor(chip, j) * 2 * rows, 2 * rows)
+        return jnp.dot(
+            tok_all[first:first + per_group, :, pl.ds(base, 2 * rows)].reshape(
+                per_group * block, 2 * rows
+            ),
+            w_gu[e, pl.ds(base, 2 * rows), pl.ds(at, tile)], preferred_element_type=F32,
+        )
+
+    def early_group(first, e):
+        def body(n, carry):
+            at = pl.multiple_of(n * tile, tile)
+            early[:, pl.ds(at, tile)] = (
+                chip_product(first, e, 0, at) + chip_product(first, e, 1, at)
+                + chip_product(first, e, 2, at)
+            )
+            return carry
+
+        lax.fori_loop(0, 2 * ff // tile, body, 0)
+
+    def hidden_group(first, e, resume=False):
         count = per_group * block
         flip[: per_group * 8] = share_in[first:first + per_group].reshape(per_group * 8, block)
         columns = flip[...].T
@@ -288,11 +306,13 @@
 
         def body(j, carry):
             at = pl.multiple_of(j * tile, tile)
-            g = jnp.dot(picked, w_gu[e, :, pl.ds(at, tile)], preferred_element_type=F32)
-            u = jnp.dot(
-                picked, w_gu[e, :, pl.ds(pl.multiple_of(ff + at, tile), tile)],
-                preferred_element_type=F32,
-            )
+            up_at = pl.multiple_of(ff + at, tile)
+            if resume:
+                g = early[:, pl.ds(at, tile)] + chip_product(first, e, 3, at)
+                u = early[:, pl.ds(up_at, tile)] + chip_product(first, e, 3, up_at)
+            else:
+                g = jnp.dot(picked, w_gu[e, :, pl.ds(at, tile)], preferred_element_type=F32)
+                u = jnp.dot(picked, w_gu[e, :, pl.ds(up_at, tile)], preferred_element_type=F32)
             value = (g / (1.0 + jnp.exp(-g))) * u * scale
             hidden[first * block:first * block + count,
                    pl.ds(pl.multiple_of(e * ff + at, tile), tile)] = value.astype(BF16)
@@ -364,7 +384,9 @@
             hidden_group(2, e)
         for j in range(chips):
             wait_sibling("gu", gu_keys[local - 1], j)
-        hidden_group(2, local - 1)
+            if j == 2:
+                early_group(2, local - 1)
+        hidden_group(2, local - 1, True)
         wait_sibling("down", down_keys, 0)
         rows_out(0, 2, 2)
         send_relay(0)
@@ -468,6 +490,7 @@
             pltpu.VMEM((128, 128), F32),
             pltpu.VMEM((parts, block, width // parts), BF16),
             pltpu.VMEM((2, block, width // parts), F32),
+            pltpu.VMEM((2 * block, 2 * ff), F32),
             dma((experts_here * halves, 2 * chips)),
             dma((experts_here * halves, 2 * chips)),
             dma((halves, 2 * chips)),

time: 69 us -> 68.3 us (0.990)
  Pallas kernels: 68.1 us -> 67.4 us
where the time goes in v8:
time: 68.3 us; the launch traced here: 68.2 us
  Pallas kernels  67.4 us (99%)
  local copies, waits for them, and re-layouts  0.75 us (1%)
    pallas_call x1, Pallas kernels, local(): pl.pallas_call(functools.partial(kernel, n_group, n_hold, capacity), out_...  67.4 us

profile of v8, /device:TPU:0, one launch (start us, length us, event | category | flops | bytes accessed | tf_op | source)
XLA Modules:
  0.0 68.2 jit_solution(10612513382035598868)
XLA Ops:
  0.0 67.4 %shard_map.73 = bf16[128,1536]{1,0:T(8,128)(2,1)S(1)} custom-call(bf16[128,1536]{1,0:T(8,128)(2,1)} %tokens_in.1, f32[2,192,512]{2,1,0:T(8,128)} %gate_in.1, f32[2,192,512]{2,1,0:T(8,128)} %up_in.1, f32[2,192,512]{2,1,0:T(8,128)} %bitcast.4, s32[6,128]{1,0:T(8,128)} %bitcast.5, f32[6,128]{1,0:T(8,128)} %bitcast.6, s32[1,128]{1,0:T(1,128)} %bitcast.7), custom_call_target="tpu_custom_call" | custom-call | tf_op jit(solution)/shard_map/pallas_call | solution.py:469
  67.5 0.7 %copy.9 = bf16[128,1536]{1,0:T(8,128)(2,1)} copy(bf16[128,1536]{1,0:T(8,128)(2,1)S(1)} %shard_map.73) | data formatting | bytes 786432

commit v9 on v8

--- a/solution.py
+++ b/solution.py
@@ -371,8 +371,9 @@
         for e in range(local):
             last = e == local - 1
             if last:
+                send_own("down", turns(down_keys)[:2])
                 service_far("gu", gu_keys[e])
-                send_own("down", turns(down_keys))
+                send_own("down", turns(down_keys)[2:])
             for j in range(chips):
                 if not last:
                     wait_sibling("gu", gu_keys[e], j)

time: 68.3 us -> 68.3 us (level)
  no operation moved by 1% of the time
where the time goes in v9:
time: 68.3 us; the launch traced here: 68.2 us
  Pallas kernels  67.4 us (99%)
  local copies, waits for them, and re-layouts  0.75 us (1%)
    pallas_call x1, Pallas kernels, local(): pl.pallas_call(functools.partial(kernel, n_group, n_hold, capacity), out_...  67.4 us

profile of v9, /device:TPU:0, one launch (start us, length us, event | category | flops | bytes accessed | tf_op | source)
XLA Modules:
  0.0 68.2 jit_solution(16045644891620983018)
XLA Ops:
  0.0 67.4 %shard_map.73 = bf16[128,1536]{1,0:T(8,128)(2,1)S(1)} custom-call(bf16[128,1536]{1,0:T(8,128)(2,1)} %tokens_in.1, f32[2,192,512]{2,1,0:T(8,128)} %gate_in.1, f32[2,192,512]{2,1,0:T(8,128)} %up_in.1, f32[2,192,512]{2,1,0:T(8,128)} %bitcast.4, s32[6,128]{1,0:T(8,128)} %bitcast.5, f32[6,128]{1,0:T(8,128)} %bitcast.6, s32[1,128]{1,0:T(1,128)} %bitcast.7), custom_call_target="tpu_custom_call" | custom-call | tf_op jit(solution)/shard_map/pallas_call | solution.py:470
  67.4 0.7 %copy.9 = bf16[128,1536]{1,0:T(8,128)(2,1)} copy(bf16[128,1536]{1,0:T(8,128)(2,1)S(1)} %shard_map.73) | data formatting | bytes 786432
